TPU v7x, 256 devices: a whole 4x4x8 slice. The times are simulated.
256 devices in a mesh: ctx: 32 (over x_lo, z, core), tp: 8 (over x_hi, y).
Axes of the slice: x: 4 (x_hi: 2, x_lo: 2; x = x_hi * 2 + x_lo), y: 4, z: 8, core: 2. Of those that a mesh axis runs over, the one named last changes fastest.
Arguments:
- queries: bfloat16 [4096, 3072], P('ctx', 'tp'), may hold values from -5 to 5
- key_rows: bfloat16 [4096, 1024], P('ctx', 'tp'), may hold values from -5 to 5
- value_rows: bfloat16 [4096, 1024], P('ctx', 'tp'), may hold values from -6 to 6
- attn_out: bfloat16 [4096, 3072], P('ctx', 'tp'), may hold values from -6 to 6
- grad_out: bfloat16 [4096, 3072], P('ctx', 'tp'), may hold values from -16 to 16
- segments: int32 [4096], replicated, may hold values from 0 to 2, never falling along the last dimension, each value on 1 to 2560 neighbouring positions
- grad_moe_out: bfloat16 [4096, 3072], P('ctx'), may hold values from -12 to 12
- expert_ids: int32 [4096, 2], P('ctx'), may hold values from 0 to 7, as said below
- route_weights: float32 [4096, 2], P('ctx'), may hold values from 0.2 to 1
- saved_gate: bfloat16 [36864, 4096], P('ctx', 'tp'), may hold values from -6 to 6
- saved_up: bfloat16 [36864, 4096], P('ctx', 'tp'), may hold values from -6 to 6
- w_gate: bfloat16 [3072, 131072], P(None, ('ctx', 'tp')), may hold values from -0.109375 to 0.109375
- w_up: bfloat16 [3072, 131072], P(None, ('ctx', 'tp')), may hold values from -0.109375 to 0.109375
- w_down: bfloat16 [131072, 3072], P(('ctx', 'tp')), may hold values from -0.046875 to 0.046875
Outputs:
- grad_queries: bfloat16 [4096, 3072], P('ctx', 'tp')
- grad_keys: bfloat16 [4096, 1024], P('ctx', 'tp')
- grad_values: bfloat16 [4096, 1024], P('ctx', 'tp')
- grad_moe_in: bfloat16 [4096, 3072], P('ctx', 'tp')
Inputs may be any that keep to these rules, and one draw needn't show every extreme that they name: `expert_ids`: A token's two ids differ. In each aligned block of 128 tokens no expert is named more than 36 times, and one expert, the same in every block, is named exactly 36 times in each block.
All inputs are finite; a program needn't handle non-finite values.
Results may differ from a plain program's by a relative error of at most 0.02.
Values may be sent and summed in bfloat16 or wider, within the bound.
A program may use at most 128 MiB of HBM per device.

v0:
```python
import jax
import jax.numpy as jnp
from jax import lax
from jax.sharding import PartitionSpec as P

EXPERTS = 8
HEAD = 128


def per_device(
    queries,
    key_rows,
    value_rows,
    attn_out,
    grad_out,
    segments,
    grad_moe_out,
    expert_ids,
    route_weights,
    saved_gate,
    saved_up,
    w_gate,
    w_up,
    w_down,
):
    ctx_count = lax.axis_size("ctx")
    local_rows = queries.shape[0]
    total_rows = ctx_count * local_rows
    kv_width = key_rows.shape[1]
    kv_heads = kv_width // HEAD
    group_size = queries.shape[1] // kv_width
    scaling = HEAD ** (-0.5)
    query_heads = queries.reshape(local_rows, kv_heads, group_size, HEAD)
    grad_heads = grad_out.reshape(local_rows, kv_heads, group_size, HEAD)
    out_heads = attn_out.reshape(local_rows, kv_heads, group_size, HEAD)
    row_dots = jnp.einsum(
        "qhgd,qhgd->hgq", grad_heads.astype(jnp.float32), out_heads.astype(jnp.float32)
    )
    first_row = lax.axis_index("ctx") * local_rows
    query_pos = first_row + jnp.arange(local_rows, dtype=jnp.int32)
    query_seg = lax.dynamic_slice_in_dim(segments, first_row, local_rows)
    key_values = jnp.concatenate([key_rows, value_rows], axis=1)
    whole_keys = lax.all_gather(key_values, "ctx", axis=0, tiled=True)
    key_part = whole_keys[:, :kv_width].reshape(whole_keys.shape[0], kv_heads, HEAD)
    scores = scaling * jnp.einsum(
        "qhgd,khd->hgqk", query_heads, key_part, preferred_element_type=jnp.float32
    )
    key_pos = jnp.arange(total_rows, dtype=jnp.int32)
    visible = (key_pos[None, :] <= query_pos[:, None]) & (segments[None, :] == query_seg[:, None])
    highest = jnp.max(jnp.where(visible, scores, -1e30), axis=-1)
    denominator = jnp.sum(jnp.where(visible, jnp.exp(scores - highest[..., None]), 0.0), axis=-1)
    logsum = highest + jnp.log(denominator)
    value_part = whole_keys[:, kv_width:].reshape(whole_keys.shape[0], kv_heads, HEAD)
    soft_weights = jnp.where(visible, jnp.exp(scores - logsum[..., None]), 0.0)
    grad_probs = jnp.einsum(
        "qhgd,khd->hgqk", grad_heads, value_part, preferred_element_type=jnp.float32
    )
    grad_scores = (soft_weights * (grad_probs - row_dots[..., None])).astype(jnp.bfloat16)
    soft_weights, grad_scores = (soft_weights, grad_scores)
    key_part = whole_keys[:, :kv_width].reshape(whole_keys.shape[0], kv_heads, HEAD)
    grad_query = scaling * jnp.einsum(
        "hgqk,khd->qhgd", grad_scores, key_part, preferred_element_type=jnp.float32
    )
    count = whole_keys.shape[0]
    grad_key = scaling * jnp.einsum(
        "hgqk,qhgd->khd", grad_scores, query_heads, preferred_element_type=jnp.float32
    )
    grad_value = jnp.einsum(
        "hgqk,qhgd->khd",
        soft_weights.astype(jnp.bfloat16),
        grad_heads,
        preferred_element_type=jnp.float32,
    )
    key_terms = jnp.concatenate(
        [grad_key.reshape(count, kv_width), grad_value.reshape(count, kv_width)], axis=1
    )
    owned_terms = lax.psum_scatter(
        key_terms.astype(jnp.bfloat16), "ctx", scatter_dimension=0, tiled=True
    ).astype(jnp.float32)
    grad_queries = grad_query.reshape(local_rows, queries.shape[1]).astype(jnp.bfloat16)
    grad_keys = owned_terms[:, :kv_width].astype(jnp.bfloat16)
    grad_values = owned_terms[:, kv_width:].astype(jnp.bfloat16)
    copies = ctx_count // EXPERTS
    capacity = saved_gate.shape[0] // ctx_count
    model_width = grad_moe_out.shape[1]
    flat_ids = expert_ids.reshape(-1)
    onehot = (flat_ids[:, None] == jnp.arange(EXPERTS, dtype=jnp.int32)[None, :]).astype(jnp.int32)
    slot_rank = jnp.sum((jnp.cumsum(onehot, axis=0) - onehot) * onehot, axis=1)
    slot_index = flat_ids * capacity + slot_rank
    selector = jnp.any(
        jnp.arange(EXPERTS * capacity, dtype=jnp.int32)[:, None, None]
        == slot_index.reshape(local_rows, 2)[None],
        axis=2,
    ).astype(jnp.bfloat16)
    packed = jnp.dot(selector, grad_moe_out, preferred_element_type=jnp.float32).astype(
        jnp.bfloat16
    )
    outgoing = jnp.broadcast_to(
        packed.reshape(EXPERTS, 1, capacity, model_width), (EXPERTS, copies, capacity, model_width)
    ).reshape(ctx_count * capacity, model_width)
    arrived = lax.all_to_all(outgoing, "ctx", split_axis=0, concat_axis=0, tiled=True)
    contract = (((1,), (1,)), ((), ()))
    gate_pre = saved_gate.astype(jnp.float32)
    up_pre = saved_up.astype(jnp.float32)
    hidden_grad = lax.dot_general(arrived, w_down, contract, preferred_element_type=jnp.float32)
    sigmoid_gate = jax.nn.sigmoid(gate_pre)
    grad_up = (hidden_grad * gate_pre * sigmoid_gate).astype(jnp.bfloat16)
    grad_gate = (
        hidden_grad * up_pre * sigmoid_gate * (1.0 + gate_pre * (1.0 - sigmoid_gate))
    ).astype(jnp.bfloat16)
    partial_rows = lax.dot_general(
        grad_gate, w_gate, contract, preferred_element_type=jnp.float32
    ) + lax.dot_general(grad_up, w_up, contract, preferred_element_type=jnp.float32)
    weight_pairs = route_weights.reshape(-1)[:, None]
    returned = lax.all_to_all(
        partial_rows.astype(jnp.bfloat16), "ctx", split_axis=0, concat_axis=0, tiled=True
    )
    per_slot = jnp.sum(
        returned.astype(jnp.float32).reshape(EXPERTS, copies, capacity, model_width), axis=1
    ).reshape(EXPERTS * capacity, model_width)
    combined = jnp.sum(
        (jnp.take(per_slot, slot_index, axis=0) * weight_pairs).reshape(local_rows, 2, model_width),
        axis=1,
    )
    grad_moe_in = lax.psum_scatter(
        combined.astype(jnp.bfloat16), "tp", scatter_dimension=1, tiled=True
    )
    return (grad_queries, grad_keys, grad_values, grad_moe_in)


def solution(mesh):
    in_specs = (
        P("ctx", "tp"),
        P("ctx", "tp"),
        P("ctx", "tp"),
        P("ctx", "tp"),
        P("ctx", "tp"),
        P(),
        P("ctx", None),
        P("ctx", None),
        P("ctx", None),
        P("ctx", "tp"),
        P("ctx", "tp"),
        P(None, ("ctx", "tp")),
        P(None, ("ctx", "tp")),
        P(("ctx", "tp"), None),
    )
    out_specs = (P("ctx", "tp"), P("ctx", "tp"), P("ctx", "tp"), P("ctx", "tp"))
    return jax.shard_map(
        per_device, mesh=mesh, in_specs=in_specs, out_specs=out_specs, check_vma=False
    )
```

profile of v0, /device:TPU:1, one launch (start us, length us, event | category | flops | bytes accessed | tf_op | source)
XLA Modules:
  0.0 592.6 jit_solution(17792065903385890267)
XLA Ops:
  7.2 0.9 copy.90
  10.3 3.0 convolution_convert_fusion
  13.3 2.6 broadcast_in_dim.44
  15.9 2.6 broadcast_in_dim.45
  18.5 184.7 %all_to_all.21 = bf16[32,36,3072]{2,1,0:T(8,128)(2,1)} all-to-all(bf16[32,36,3072]{2,1,0:T(8,128)(2,1)S(1)} %bitcast.104), channel_id=1, replica_groups=mesh['ctx'=32,'tp'=8] {'ctx'}, dimensions={0} | all-to-all | bytes 14155776 | tf_op jit(solution)/shard_map/all_to_all | solution.py:101
  203.2 8.8 %all_to_all.16 = bf16[1152,3072]{1,0:T(8,128)(2,1)} reshape(bf16[32,36,3072]{2,1,0:T(8,128)(2,1)} %all_to_all.21) | data formatting | bytes 14155776 | tf_op jit(solution)/shard_map/all_to_all | solution.py:101
  211.9 7.2 %fusion.44 = f32[1152,512]{1,0:T(8,128)S(1)} fusion(bf16[1152,3072]{1,0:T(8,128)(2,1)} %all_to_all.16, bf16[512,3072]{1,0:T(8,128)(2,1)} %param.27), kind=kOutput, calls=%fused_computation.74 | convolution fusion | flops 3623878656 | bytes 12582912 | tf_op jit(solution)/shard_map/dot_general | solution.py:105
  219.1 1.4 copy-done.16
  220.6 7.9 %fusion.28 = f32[1152,3072]{1,0:T(8,128)} fusion(bf16[3072,512]{1,0:T(8,128)(2,1)S(1)} %copy-done, bf16[1152,512]{1,0:T(8,128)(2,1)S(1)} %copy-done.15, f32[1152,512]{1,0:T(8,128)S(1)} %fusion.44, bf16[1152,512]{1,0:T(8,128)(2,1)S(1)} %copy-done.14), kind=kOutput, calls=%fused_computation.43 | convolution fusion | flops 3630956544 | bytes 22020096 | tf_op jit(solution)/shard_map/dot_general | solution.py:111
  228.5 10.2 %add_convert_fusion = bf16[1152,3072]{1,0:T(8,128)(2,1)} fusion(f32[1152,3072]{1,0:T(8,128)} %fusion.28, bf16[3072,512]{1,0:T(8,128)(2,1)S(1)} %copy-done.12, f32[1152,512]{1,0:T(8,128)} %copy-done.16, bf16[1152,512]{1,0:T(8,128)(2,1)} %param.23), kind=kOutput, calls=%fused_computation.2 | convolution fusion | flops 3635085312 | bytes 27918336 | tf_op jit(solution)/shard_map/dot_general | solution.py:113
  238.6 8.7 %all_to_all.17 = bf16[32,36,3072]{2,1,0:T(8,128)(2,1)} reshape(bf16[1152,3072]{1,0:T(8,128)(2,1)} %add_convert_fusion) | data formatting | bytes 14155776 | tf_op jit(solution)/shard_map/all_to_all | solution.py:115
  247.4 7.0 %all-to-all-start.1 = ((bf16[32,36,3072]{2,1,0:T(8,128)(2,1)}), bf16[32,36,3072]{2,1,0:T(8,128)(2,1)}, u32[]{:S(2)}, u32[]{:S(2)}) async-start(bf16[32,36,3072]{2,1,0:T(8,128)(2,1)} %all_to_all.17), calls=%async_computation.1 | async-start | bytes 15728640 | tf_op jit(solution)/shard_map/all_to_all | solution.py:115
  255.9 1.9 fusion.26
  257.8 95.4 %all-gather.2.cloned.1.call-done = bf16[4096,256]{1,0:T(8,128)(2,1)} async-done(((bf16[128,256]{1,0:T(8,128)(2,1)}), bf16[4096,256]{1,0:T(8,128)(2,1)}) %all-gather.2.cloned.1.call-update) | async-done | bytes 2097168 | tf_op jit(solution)/shard_map/all_gather | solution.py:43
  353.2 2.5 fusion.2
  355.7 1.2 fusion.5
  357.3 2.0 fusion.8
  359.2 1.1 fusion.11
  360.9 1.3 fusion.12
  362.4 2.5 copy.115
  366.8 72.2 %all-to-all-done.1 = bf16[32,36,3072]{2,1,0:T(8,128)(2,1)} async-done(((bf16[32,36,3072]{2,1,0:T(8,128)(2,1)}), bf16[32,36,3072]{2,1,0:T(8,128)(2,1)}, u32[]{:S(2)}, u32[]{:S(2)}) %all-to-all-start.1) | async-done | bytes 7077920 | tf_op jit(solution)/shard_map/all_to_all | solution.py:115
  439.0 7.0 %convert_reduce_fusion = f32[8,36,3072]{2,1,0:T(8,128)} fusion(bf16[32,36,3072]{2,1,0:T(8,128)(2,1)} %all-to-all-done.1), kind=kLoop, calls=%fused_computation.1 | loop fusion | flops 6193152 | bytes 10616832 | tf_op jit(solution)/shard_map/reduce_sum | solution.py:118
  446.0 2.3 reshape.188
  448.4 3.5 gather_fusion
  451.9 3.8 gather.7
  455.7 6.5 %multiply_reduce_fusion = bf16[128,3072]{1,0:T(8,128)(2,1)} fusion(f32[128,2,3072]{2,1,0:T(2,128)S(1)} %gather.7, pred[128,2]{1,0:T(8,128)(4,1)S(1)} %copy.93, f32[128,2]{1,0:T(8,128)S(1)} %copy-done.3), kind=kLoop, calls=%fused_computation.28 | loop fusion | flops 1966080 | bytes 3933440 | tf_op jit(solution)/shard_map/reduce_sum | solution.py:121
  462.2 2.4 copy.117
  464.7 3.0 fusion.32
  468.4 36.4 %reduce-scatter.7.cloned.1.call-done = bf16[128,256]{1,0:T(8,128)(2,1)} async-done(((bf16[4096,256]{1,0:T(8,128)(2,1)}), bf16[128,256]{1,0:T(8,128)(2,1)}) %reduce-scatter.7.cloned.1.call-update) | async-done | bytes 65552
  504.8 1.4 fusion.43
  506.2 78.2 %reduce-scatter.9.cloned.1.call-done = bf16[384,128]{1,0:T(8,128)(2,1)} async-done(((bf16[3072,128]{1,0:T(8,128)(2,1)}), bf16[384,128]{1,0:T(8,128)(2,1)}) %reduce-scatter.9.cloned.1.call-update) | async-done | bytes 98320
  584.4 1.6 copy.118
  (68 shorter events, 7.3 us)
Async XLA Ops:
  7.2 213.4 %copy-start = (bf16[3072,512]{1,0:T(8,128)(2,1)S(1)}, bf16[3072,512]{1,0:T(8,128)(2,1)}, u32[]{:S(2)}) copy-start(bf16[3072,512]{1,0:T(8,128)(2,1)} %param.25) | copy-start | bytes 9437188
  211.9 8.6 %copy-start.14 = (bf16[1152,512]{1,0:T(8,128)(2,1)S(1)}, bf16[1152,512]{1,0:T(8,128)(2,1)}, u32[]{:S(2)}) copy-start(bf16[1152,512]{1,0:T(8,128)(2,1)} %param.24) | copy-start | bytes 3538948
  211.9 8.6 %copy-start.15 = (bf16[1152,512]{1,0:T(8,128)(2,1)S(1)}, bf16[1152,512]{1,0:T(8,128)(2,1)}, u32[]{:S(2)}) copy-start(bf16[1152,512]{1,0:T(8,128)(2,1)} %param.23) | copy-start | bytes 3538948
  219.1 1.5 copy-start.16
  220.6 7.9 %copy-start.12 = (bf16[3072,512]{1,0:T(8,128)(2,1)S(1)}, bf16[3072,512]{1,0:T(8,128)(2,1)}, u32[]{:S(2)}) copy-start(bf16[3072,512]{1,0:T(8,128)(2,1)} %param.26) | copy-start | bytes 9437188
  247.4 7.1 %copy-start.7 = (bf16[128,128]{1,0:T(8,128)(2,1)S(1)}, bf16[128,128]{1,0:T(8,128)(2,1)}, u32[]{:S(2)}) copy-start(bf16[128,128]{1,0:T(8,128)(2,1)} %param.16) | copy-start | bytes 98308
  247.4 7.1 %copy-start.8 = (bf16[128,128]{1,0:T(8,128)(2,1)S(1)}, bf16[128,128]{1,0:T(8,128)(2,1)}, u32[]{:S(2)}) copy-start(bf16[128,128]{1,0:T(8,128)(2,1)} %param.15) | copy-start | bytes 98308
  247.4 8.0 %copy-start.4 = (bf16[128,384]{1,0:T(8,128)(2,1)S(1)}, bf16[128,384]{1,0:T(8,128)(2,1)}, u32[]{:S(2)}) copy-start(bf16[128,384]{1,0:T(8,128)(2,1)} %param.14) | copy-start | bytes 294916
  247.4 8.1 %copy-start.5 = (bf16[128,384]{1,0:T(8,128)(2,1)S(1)}, bf16[128,384]{1,0:T(8,128)(2,1)}, u32[]{:S(2)}) copy-start(bf16[128,384]{1,0:T(8,128)(2,1)} %param.18) | copy-start | bytes 294916
  247.4 8.3 %copy-start.6 = (bf16[128,384]{1,0:T(8,128)(2,1)S(1)}, bf16[128,384]{1,0:T(8,128)(2,1)}, u32[]{:S(2)}) copy-start(bf16[128,384]{1,0:T(8,128)(2,1)} %param.17) | copy-start | bytes 294916
  247.4 8.4 %copy-start.9 = (s32[4096]{0:T(1024)S(1)}, s32[4096]{0:T(1024)}, u32[]{:S(2)}) copy-start(s32[4096]{0:T(1024)} %param.19) | copy-start | bytes 49156
  247.4 191.6 %all-to-all-start.1 = ((bf16[32,36,3072]{2,1,0:T(8,128)(2,1)}), bf16[32,36,3072]{2,1,0:T(8,128)(2,1)}, u32[]{:S(2)}, u32[]{:S(2)}) async-start(bf16[32,36,3072]{2,1,0:T(8,128)(2,1)} %all_to_all.17), calls=%async_computation.1 | async-start | bytes 15728640 | tf_op jit(solution)/shard_map/all_to_all | solution.py:115
  254.4 98.8 %all-gather.2.cloned.1.call-start = ((), (), s32[]{:S(2)}) async-start(), calls=%async_computation.4 | async-start | bytes 2162688 | tf_op jit(solution)/shard_map/all_gather | solution.py:43
  255.1 249.7 %reduce-scatter.7.cloned.1.call-start = ((), (), s32[]{:S(2)}) async-start(), calls=%async_computation.5 | async-start | bytes 2162688
  355.7 1.6 copy-start.13
  359.2 1.7 copy-start.2
  362.4 2.6 copy-start.10
  362.4 3.0 copy-start.11
  364.9 219.5 %reduce-scatter.9.cloned.1.call-start = ((), (), s32[]{:S(2)}) async-start(), calls=%async_computation.6 | async-start | bytes 884736
  451.9 3.8 copy-start.3
  462.2 123.9 %copy-start.1 = (bf16[3072,512]{1,0:T(8,128)(2,1)S(1)}, bf16[3072,512]{1,0:T(8,128)(2,1)}, u32[]{:S(2)}) copy-start(bf16[3072,512]{1,0:T(8,128)(2,1)} %param.25) | copy-start | bytes 9437188
Sparse Core Ops, SparseCore 0:
  257.6 95.5 all-gather.1
  365.1 139.6 reduce-scatter.6
  509.2 75.2 reduce-scatter.8
where the time goes:
time: 594 us; the launch traced here: 593 us
  waiting for transfers between devices  282 us (47%)
  blocking collectives  185 us (31%)
  local copies, waits for them, and re-layouts  46.7 us (8%)
  matrix products  38 us (6%)
  other arithmetic  19.6 us (3%)
  between operations  14.1 us (2%)
  starting transfers between devices  7.28 us (1%)
    all_to_all x1, blocking collectives, per_device(): lax.all_to_all(outgoing, 'ctx', split_axis=0, concat_axis=0, tiled=True)  185 us
    unnamed x5, waiting for transfers between devices  115 us
    all_gather x1, waiting for transfers between devices, per_device(): whole_keys = lax.all_gather(key_values, 'ctx', axis=0, tiled=True)  95.4 us
    all_to_all x1, waiting for transfers between devices, per_device(): lax.all_to_all(partial_rows.astype(jnp.bfloat16), 'ctx', split_axis=0, co...  72.2 us
  transfers between devices with their start and end apart: 4, of which 4 were waited for; matrix products, arithmetic and copies ran while one was open for 8% of the time, Pallas kernels for 0%

commit v1 on v0

v1 whole, which is shorter than its diff:
```python
import jax
import jax.numpy as jnp
from jax import lax
from jax.experimental import pallas as pl
from jax.experimental.pallas import tpu as pltpu
from jax.sharding import PartitionSpec as P

EXPERTS = 8
HEAD = 128
CAP = 36
PAD = 48
CT = 128
N_CTX = 32
HEADS = 3
WINDOW = 10
CHIPS = 16
SUBS = 3
SUB = 96
BLOCK = 288
COLS = 384
HALF = 1536
WIDE = 3072
HID = 512
MESH = pl.DeviceIdType.MESH
F32 = jnp.float32
BF16 = jnp.bfloat16
NT = (((1,), (1,)), ((), ()))
NN = (((1,), (0,)), ((), ()))
TN = (((0,), (0,)), ((), ()))


def dot(a, b, dims):
    return lax.dot_general(a, b, dims, preferred_element_type=F32)


def kernel(
    q_ref, k_ref, v_ref, ao_ref, go_ref, seg_ref, gm_ref, ids_ref, rw_ref,
    sg_ref, su_ref, wg_ref, wu_ref, wd_ref,
    dq_ref, dk_ref, dv_ref, dm_ref,
    kv, st, q3, g3, dkv, dks, dacc,
    gm, packed, arrive, arr, sg, su, wg, wu, wd,
    part, sib, b1, b2, b3s, b3, fin, unpacked, ret,
    ld_sem, kv_s, kv_r, kf_s, kf_r, ds_s, ds_r, da_s, da_r,
    pa_s, pa_r, g1_s, g1_r, g2_s, g2_r, g3_s, g3_r, g4_s, g4_r,
    r0_s, r0_r, r1_s, r1_r, r2_s, r2_r, r3_s, r3_r, pr_s, pr_r,
):
    c = lax.axis_index("ctx")
    u = lax.axis_index("tp")
    core = c % 2
    chip = c // 2
    zp = chip % 2
    xh = u // 4
    y = u % 4
    quarter = c % 4
    sibling = (c + 1 - 2 * core, u)
    first = (c + core * (2 - 4 * zp), u + (1 - core) * (4 - 8 * xh))
    last = (c + (1 - core) * (2 - 4 * zp), u + core * (4 - 8 * xh))

    def along_y(dy):
        return (c, xh * 4 + (y + dy) % 4)

    def send(src, dst, ss, rs, to):
        pltpu.make_async_remote_copy(
            src_ref=src, dst_ref=dst, send_sem=ss, recv_sem=rs,
            device_id=to, device_id_type=MESH,
        ).start()

    def got(dst, ss, rs):
        pltpu.make_async_remote_copy(
            src_ref=dst, dst_ref=dst, send_sem=ss, recv_sem=rs,
            device_id=sibling, device_id_type=MESH,
        ).wait_recv()

    def sent(src, ss, rs):
        pltpu.make_async_remote_copy(
            src_ref=src, dst_ref=src, send_sem=ss, recv_sem=rs,
            device_id=sibling, device_id_type=MESH,
        ).wait_send()

    barrier = pltpu.get_barrier_semaphore()

    @pl.loop(0, N_CTX)
    def _(i):
        @pl.when(i != c)
        def _():
            pl.semaphore_signal(barrier, inc=1, device_id=(i, u), device_id_type=MESH)

    for dy in (1, 2, 3):
        pl.semaphore_signal(barrier, inc=1, device_id=along_y(dy), device_id_type=MESH)
    pl.semaphore_signal(
        barrier, inc=1, device_id=(c, u + 4 - 8 * xh), device_id_type=MESH
    )

    own_cols = pl.ds(pl.multiple_of(u * COLS, 128), COLS)
    loads = [
        (gm_ref.at[:, own_cols], gm),
        (wd_ref, wd),
        (sg_ref, sg),
        (su_ref, su),
        (wg_ref, wg),
        (wu_ref, wu),
    ]

    def load(i):
        return pltpu.make_async_copy(loads[i][0], loads[i][1], ld_sem.at[i])

    for i in range(len(loads)):
        load(i).start()

    lane = lax.broadcasted_iota(jnp.int32, (CT, CT), 1)
    sub = lax.broadcasted_iota(jnp.int32, (CT, CT), 0)
    ids = ids_ref[...]
    hot = [(ids[:, k : k + 1] == lane).astype(F32) for k in range(2)]
    before = (lane < sub).astype(BF16)
    count = dot(before, (hot[0] + hot[1]).astype(BF16), NN)
    place = count + (PAD * lane).astype(F32)
    slot_lane = lax.broadcasted_iota(jnp.int32, (CT, EXPERTS * PAD), 1)
    pick = []
    for k in range(2):
        slot = jnp.sum(hot[k] * place, axis=1, keepdims=True).astype(jnp.int32)
        pick.append((slot_lane == slot).astype(F32))
    selector = jnp.transpose(pick[0] + pick[1]).astype(BF16)
    load(0).wait()
    packed[...] = dot(selector, gm[...], NN).astype(BF16).reshape(EXPERTS, PAD, COLS)
    kv[0, core, :, :HEAD] = k_ref[...]
    kv[0, core, :, HEAD:] = v_ref[...]

    pl.semaphore_wait(barrier, N_CTX - 1 + 4)

    source_part = c // 8
    source_slot = c % 8
    expert = c // 4

    @pl.loop(0, EXPERTS)
    def _(e):
        to = 4 * e + source_part

        @pl.when(to == c)
        def _():
            pltpu.make_async_copy(
                packed.at[e], arrive.at[source_slot], pa_r.at[source_slot]
            ).start()

        @pl.when(to != c)
        def _():
            send(packed.at[e], arrive.at[source_slot], pa_s.at[e], pa_r.at[source_slot], (to, u))

    later = jnp.minimum(WINDOW, CHIPS - 1 - chip) + 1
    earlier = jnp.minimum(WINDOW, chip) + 1

    send(kv.at[0, core], kv.at[0, core], kf_s.at[0], kf_r.at[0], sibling)

    @pl.loop(1, later)
    def _(d):
        send(kv.at[0, core], kv.at[d, core], kv_s.at[d], kv_r.at[d], (c + 2 * d, u))

    q3[...] = jnp.concatenate([q_ref[:, h * HEAD : (h + 1) * HEAD] for h in range(HEADS)], axis=0)
    g3[...] = jnp.concatenate([go_ref[:, h * HEAD : (h + 1) * HEAD] for h in range(HEADS)], axis=0)
    a3 = jnp.concatenate([ao_ref[:, h * HEAD : (h + 1) * HEAD] for h in range(HEADS)], axis=0)
    row_dots = jnp.sum(
        jnp.transpose(g3[...].astype(F32) * a3.astype(F32)), axis=0, keepdims=True
    )
    segs = seg_ref[...]
    starts = [
        jnp.sum((segs < k).astype(F32)).astype(jnp.int32) for k in (1, 2)
    ]
    own_seg = seg_ref[pl.ds(c, 1), :]
    start = jnp.where(own_seg == 0, 0, jnp.where(own_seg == 1, starts[0], starts[1]))
    start = jnp.concatenate([start] * HEADS, axis=1)
    own_pos = c * CT + lax.broadcasted_iota(jnp.int32, (1, CT), 1)
    own_pos = jnp.concatenate([own_pos] * HEADS, axis=1)

    @pl.loop(0, 8)
    def _(i):
        got(arrive.at[i], pa_s.at[i], pa_r.at[i])

    def dense_map(shape, row_axis):
        rows = lax.broadcasted_iota(jnp.int32, shape, row_axis)
        slots = lax.broadcasted_iota(jnp.int32, shape, 1 - row_axis)
        block = sum((rows >= CAP * i).astype(jnp.int32) for i in range(1, 8))
        return (slots == rows + (PAD - CAP) * block).astype(BF16)

    arr[quarter, :, own_cols] = dot(
        dense_map((BLOCK, 8 * PAD), 0), arrive[...].reshape(8 * PAD, COLS), NN
    ).astype(BF16)

    def at_block(k, fr, lr):
        dz = lr * (1 - k) + fr * k
        dx = fr * (1 - k) + lr * k
        return 2 * (zp + dz * (1 - 2 * zp)) + k, xh + dx * (1 - 2 * xh)

    def block(ref, s, k, fr, lr):
        row, col = at_block(k, fr, lr)
        return ref.at[row, pl.ds(s * SUB, SUB), pl.ds(pl.multiple_of(col * HALF, 128), HALF)]

    def piece(ref, s, fr, py):
        row, col = at_block(core, fr, 0)
        return ref.at[
            row, pl.ds(s * SUB, SUB), pl.ds(pl.multiple_of(col * HALF + py * COLS, 128), COLS)
        ]

    def gather_1(s):
        own = piece(arr, s, 0, y)
        send(own, own, g1_s.at[s], g1_r.at[s], first)
        for dy in (1, 2, 3):
            send(own, own, g2_s.at[s, 0, dy], g2_r.at[s, 0, dy], along_y(dy))

    def gather_2(s):
        other = piece(arr, s, 1, y)
        got(other, g1_s.at[s], g1_r.at[s])
        for dy in (1, 2, 3):
            send(other, other, g2_s.at[s, 1, dy], g2_r.at[s, 1, dy], along_y(dy))

    def gather_3(s):
        for fr in (0, 1):
            for dy in (1, 2, 3):
                got(piece(arr, s, fr, (y + 4 - dy) % 4), g2_s.at[s, fr, dy], g2_r.at[s, fr, dy])
            whole = block(arr, s, core, fr, 0)
            send(whole, whole, g3_s.at[s, fr], g3_r.at[s, fr], last)
            send(whole, whole, g4_s.at[s, fr, 0], g4_r.at[s, fr, 0], sibling)

    def gather_4(s):
        for fr in (0, 1):
            whole = block(arr, s, core, fr, 1)
            got(whole, g3_s.at[s, fr], g3_r.at[s, fr])
            send(whole, whole, g4_s.at[s, fr, 1], g4_r.at[s, fr, 1], sibling)

    def gather_5(s):
        for fr in (0, 1):
            for lr in (0, 1):
                got(block(arr, s, 1 - core, fr, lr), g4_s.at[s, fr, lr], g4_r.at[s, fr, lr])

    def expert_rows(s):
        rows = pl.ds(s * SUB, SUB)
        hidden = dot(arr[:, rows, :].reshape(4 * SUB, WIDE), wd[...], NT)
        gate = sg[:, rows, :].reshape(4 * SUB, HID).astype(F32)
        up = su[:, rows, :].reshape(4 * SUB, HID).astype(F32)
        sig = jax.nn.sigmoid(gate)
        hs = hidden * sig
        grad_up = (hs * gate).astype(BF16)
        grad_gate = (hs * up * (1.0 + gate * (1.0 - sig))).astype(BF16)

        @pl.loop(0, WIDE // HID)
        def _(n):
            cols = pl.ds(pl.multiple_of(n * HID, HID), HID)
            out = dot(grad_gate, wg[cols, :], NT) + dot(grad_up, wu[cols, :], NT)
            part[:, rows, cols] = out.astype(BF16).reshape(4, SUB, HID)

    def return_0(s):
        for i in (0, 1):
            send(
                part.at[2 * i + 1 - core, pl.ds(s * SUB, SUB)],
                sib.at[i, pl.ds(s * SUB, SUB)],
                r0_s.at[s, i], r0_r.at[s, i], sibling,
            )

    def sib_block(s, fr, lr):
        row, col = at_block(core, fr, lr)
        return sib[
            row // 2, pl.ds(s * SUB, SUB), pl.ds(pl.multiple_of(col * HALF, 128), HALF)
        ].astype(F32)

    def return_1(s):
        for i in (0, 1):
            got(sib.at[i, pl.ds(s * SUB, SUB)], r0_s.at[s, i], r0_r.at[s, i])
        for fr in (1, 0):
            mine = block(part, s, core, fr, 1)
            mine[...] = (mine[...].astype(F32) + sib_block(s, fr, 1)).astype(BF16)
            send(mine, b1.at[s, fr], r1_s.at[s, fr], r1_r.at[s, fr], last)

    def return_2(s):
        for fr in (1, 0):
            got(b1.at[s, fr], r1_s.at[s, fr], r1_r.at[s, fr])
            mine = block(part, s, core, fr, 0)
            mine[...] = (
                mine[...].astype(F32) + sib_block(s, fr, 0) + b1[s, fr].astype(F32)
            ).astype(BF16)
            for dy in (1, 2, 3):
                send(
                    piece(part, s, fr, (y + dy) % 4), b2.at[s, fr, dy - 1],
                    r2_s.at[s, fr, dy], r2_r.at[s, fr, dy], along_y(dy),
                )

    def y_sum(s, fr):
        for dy in (1, 2, 3):
            got(b2.at[s, fr, dy - 1], r2_s.at[s, fr, dy], r2_r.at[s, fr, dy])
        total = piece(part, s, fr, y)[...].astype(F32)
        for i in range(3):
            total = total + b2[s, fr, i].astype(F32)
        return total

    def return_3(s):
        b3s[s] = y_sum(s, 1).astype(BF16)
        send(b3s.at[s], b3.at[s], r3_s.at[s], r3_r.at[s], first)

    def return_4(s):
        total = y_sum(s, 0)
        got(b3.at[s], r3_s.at[s], r3_r.at[s])
        fin[pl.ds(s * SUB, SUB), :] = (total + b3[s].astype(F32)).astype(BF16)

    def keys_forward():
        @pl.loop(1, earlier)
        def _(d):
            mine = kv.at[d, core]
            got(mine, kv_s.at[d], kv_r.at[d])
            send(mine, mine, kf_s.at[d], kf_r.at[d], sibling)

    def keys_of(d):
        return kv[d, :, :, :HEAD].reshape(2 * CT, HEAD)

    def scores_pass():
        def step(d, top):
            got(kv.at[d, 1 - core], kf_s.at[d], kf_r.at[d])
            s = dot(keys_of(d), q3[...], NT) * (HEAD ** -0.5)
            pos = (chip - d) * 2 * CT + lax.broadcasted_iota(jnp.int32, (2 * CT, 1), 0)
            s = jnp.where((pos <= own_pos) & (pos >= start), s, -1e30)
            st[d] = s
            return jnp.maximum(top, jnp.max(s, axis=0, keepdims=True))

        top = lax.fori_loop(0, earlier, step, jnp.full((1, HEADS * CT), -1e30, F32))

        def step_2(d, total):
            p = jnp.exp(st[d] - top)
            st[d] = p
            return total + jnp.sum(p, axis=0, keepdims=True)

        total = lax.fori_loop(0, earlier, step_2, jnp.zeros((1, HEADS * CT), F32))
        return 1.0 / total

    def grads_pass(inverse):
        def step(d, dqt):
            probs = st[d] * inverse
            keys = keys_of(d)
            values = kv[d, :, :, HEAD:].reshape(2 * CT, HEAD)
            grad_probs = dot(values, g3[...], NT)
            grad_scores = (probs * (grad_probs - row_dots)).astype(BF16)
            dkv[d, :, :, :HEAD] = (
                (dot(grad_scores, q3[...], NN) * (HEAD ** -0.5)).astype(BF16).reshape(2, CT, HEAD)
            )
            dkv[d, :, :, HEAD:] = (
                dot(probs.astype(BF16), g3[...], NN).astype(BF16).reshape(2, CT, HEAD)
            )
            send(dkv.at[d, 1 - core], dks.at[d], ds_s.at[d], ds_r.at[d], sibling)
            return dqt + dot(keys, grad_scores, TN)

        dqt = lax.fori_loop(0, earlier, step, jnp.zeros((HEAD, HEADS * CT), F32))
        dq = jnp.transpose(dqt * (HEAD ** -0.5)).astype(BF16)
        for h in range(HEADS):
            dq_ref[:, h * HEAD : (h + 1) * HEAD] = dq[h * CT : (h + 1) * CT, :]

    def keys_return():
        @pl.loop(0, earlier)
        def _(d):
            got(dks.at[d], ds_s.at[d], ds_r.at[d])
            dkv[d, core] = (dkv[d, core].astype(F32) + dks[d].astype(F32)).astype(BF16)

            @pl.when(d > 0)
            def _():
                send(dkv.at[d, core], dacc.at[d], da_s.at[d], da_r.at[d], (c - 2 * d, u))

    def keys_finish():
        def step(d, total):
            got(dacc.at[d], da_s.at[d], da_r.at[d])
            return total + dacc[d].astype(F32)

        total = lax.fori_loop(1, later, step, dkv[0, core].astype(F32))
        dk_ref[...] = total[:, :HEAD].astype(BF16)
        dv_ref[...] = total[:, HEAD:].astype(BF16)

    for s in range(SUBS):
        gather_1(s)
    keys_forward()
    for s in range(SUBS):
        gather_2(s)
    inverse = scores_pass()
    gather_3(0)
    grads_pass(inverse)
    gather_3(1)
    gather_4(0)
    for i in range(1, 6):
        load(i).wait()
    gather_5(0)
    expert_rows(0)
    return_0(0)
    gather_3(2)
    gather_4(1)
    keys_return()
    gather_5(1)
    expert_rows(1)
    return_0(1)
    gather_4(2)
    return_1(0)
    gather_5(2)
    expert_rows(2)
    return_0(2)
    return_1(1)
    return_2(0)
    return_1(2)
    return_2(1)
    return_3(0)
    return_2(2)
    return_4(0)
    return_3(1)
    return_4(1)
    return_3(2)
    keys_finish()
    return_4(2)

    unpacked[...] = (
        dot(dense_map((8 * PAD, BLOCK), 1), fin[...], NN).astype(BF16).reshape(8, PAD, COLS)
    )

    @pl.loop(0, 8)
    def _(i):
        to = 8 * quarter + i

        @pl.when(to == c)
        def _():
            pltpu.make_async_copy(unpacked.at[i], ret.at[expert], pr_r.at[expert]).start()

        @pl.when(to != c)
        def _():
            send(unpacked.at[i], ret.at[expert], pr_s.at[i], pr_r.at[expert], (to, u))

    for s in range(SUBS):
        sent(piece(arr, s, 0, y), g1_s.at[s], g1_r.at[s])
        sent(b3s.at[s], r3_s.at[s], r3_r.at[s])
        for fr in (0, 1):
            for dy in (1, 2, 3):
                sent(piece(arr, s, fr, y), g2_s.at[s, fr, dy], g2_r.at[s, fr, dy])
                sent(b2.at[s, fr, dy - 1], r2_s.at[s, fr, dy], r2_r.at[s, fr, dy])
            sent(b1.at[s, fr], g3_s.at[s, fr], g3_r.at[s, fr])
            sent(b1.at[s, fr], r1_s.at[s, fr], r1_r.at[s, fr])
            sent(sib.at[fr, pl.ds(s * SUB, SUB)], r0_s.at[s, fr], r0_r.at[s, fr])
            for lr in (0, 1):
                sent(b1.at[s, fr], g4_s.at[s, fr, lr], g4_r.at[s, fr, lr])
    sent(kv.at[0, core], kf_s.at[0], kf_r.at[0])
    sent(dkv.at[0, core], ds_s.at[0], ds_r.at[0])

    @pl.loop(1, later)
    def _(d):
        sent(kv.at[0, core], kv_s.at[d], kv_r.at[d])

    @pl.loop(1, earlier)
    def _(d):
        sent(kv.at[d, core], kf_s.at[d], kf_r.at[d])
        sent(dkv.at[d, 1 - core], ds_s.at[d], ds_r.at[d])
        sent(dkv.at[d, core], da_s.at[d], da_r.at[d])

    @pl.loop(0, 8)
    def _(i):
        @pl.when(4 * i + source_part != c)
        def _():
            sent(packed.at[i], pa_s.at[i], pa_r.at[i])

        @pl.when(8 * quarter + i != c)
        def _():
            sent(unpacked.at[i], pr_s.at[i], pr_r.at[i])

    @pl.loop(0, EXPERTS)
    def _(i):
        got(ret.at[i], pr_s.at[i], pr_r.at[i])

    rows = ret[...].reshape(EXPERTS * PAD, COLS)
    weights = rw_ref[...]
    dm_ref[...] = sum(
        weights[:, k : k + 1] * dot(pick[k].astype(BF16), rows, NN) for k in range(2)
    ).astype(BF16)


def per_device(
    queries, key_rows, value_rows, attn_out, grad_out, segments, grad_moe_out,
    expert_ids, route_weights, saved_gate, saved_up, w_gate, w_up, w_down,
):
    vmem = pl.BlockSpec(memory_space=pltpu.VMEM)
    hbm = pl.BlockSpec(memory_space=pl.ANY)
    dma = pltpu.SemaphoreType.DMA
    slots = WINDOW + 1
    shapes = [
        jax.ShapeDtypeStruct((CT, HEADS * HEAD), BF16),
        jax.ShapeDtypeStruct((CT, HEAD), BF16),
        jax.ShapeDtypeStruct((CT, HEAD), BF16),
        jax.ShapeDtypeStruct((CT, COLS), BF16),
    ]
    scratch = [
        pltpu.VMEM((slots, 2, CT, 2 * HEAD), BF16),
        pltpu.VMEM((slots, 2 * CT, HEADS * CT), F32),
        pltpu.VMEM((HEADS * CT, HEAD), BF16),
        pltpu.VMEM((HEADS * CT, HEAD), BF16),
        pltpu.VMEM((slots, 2, CT, 2 * HEAD), BF16),
        pltpu.VMEM((slots, CT, 2 * HEAD), BF16),
        pltpu.VMEM((slots, CT, 2 * HEAD), BF16),
        pltpu.VMEM((CT, COLS), BF16),
        pltpu.VMEM((EXPERTS, PAD, COLS), BF16),
        pltpu.VMEM((8, PAD, COLS), BF16),
        pltpu.VMEM((4, BLOCK, WIDE), BF16),
        pltpu.VMEM((4, BLOCK, HID), BF16),
        pltpu.VMEM((4, BLOCK, HID), BF16),
        pltpu.VMEM((WIDE, HID), BF16),
        pltpu.VMEM((WIDE, HID), BF16),
        pltpu.VMEM((HID, WIDE), BF16),
        pltpu.VMEM((4, BLOCK, WIDE), BF16),
        pltpu.VMEM((2, BLOCK, WIDE), BF16),
        pltpu.VMEM((SUBS, 2, SUB, HALF), BF16),
        pltpu.VMEM((SUBS, 2, 3, SUB, COLS), BF16),
        pltpu.VMEM((SUBS, SUB, COLS), BF16),
        pltpu.VMEM((SUBS, SUB, COLS), BF16),
        pltpu.VMEM((BLOCK, COLS), BF16),
        pltpu.VMEM((8, PAD, COLS), BF16),
        pltpu.VMEM((EXPERTS, PAD, COLS), BF16),
        dma((6,)),
    ]
    for shape in (
        (slots,), (slots,), (slots,), (slots,),
        (8,),
        (SUBS,), (SUBS, 2, 4), (SUBS, 2), (SUBS, 2, 2),
        (SUBS, 2), (SUBS, 2), (SUBS, 2, 4), (SUBS,),
        (8,),
    ):
        scratch += [dma(shape), dma(shape)]
    return pl.pallas_call(
        kernel,
        out_shape=shapes,
        in_specs=[vmem] * 6 + [hbm] + [vmem] * 2 + [hbm] * 5,
        out_specs=[vmem] * 4,
        scratch_shapes=scratch,
        compiler_params=pltpu.CompilerParams(
            collective_id=0, has_side_effects=True, vmem_limit_bytes=60 * 2**20
        ),
        cost_estimate=pl.CostEstimate(
            flops=13 * 10**9, bytes_accessed=12 * 10**6, transcendentals=2 * 10**6
        ),
    )(
        queries, key_rows, value_rows, attn_out, grad_out,
        segments.reshape(N_CTX, CT), grad_moe_out, expert_ids, route_weights,
        saved_gate.reshape(4, BLOCK, HID), saved_up.reshape(4, BLOCK, HID),
        w_gate, w_up, w_down,
    )


def solution(mesh):
    in_specs = (
        P("ctx", "tp"), P("ctx", "tp"), P("ctx", "tp"), P("ctx", "tp"), P("ctx", "tp"),
        P(), P("ctx", None), P("ctx", None), P("ctx", None),
        P("ctx", "tp"), P("ctx", "tp"),
        P(None, ("ctx", "tp")), P(None, ("ctx", "tp")), P(("ctx", "tp"), None),
    )
    out_specs = (P("ctx", "tp"), P("ctx", "tp"), P("ctx", "tp"), P("ctx", "tp"))
    return jax.shard_map(
        per_device, mesh=mesh, in_specs=in_specs, out_specs=out_specs, check_vma=False
    )
```

time: 594 us -> 131 us (0.22)
  waiting for transfers between devices: 282 us -> 0 us
  blocking collectives: 185 us -> 0 us
  Pallas kernels: 0 us -> 121 us
  local copies, waits for them, and re-layouts: 46.7 us -> 8.66 us
  matrix products: 38 us -> 0 us
  other arithmetic: 19.6 us -> 0 us
  between operations: 14.1 us -> 0.64 us
  starting transfers between devices: 7.28 us -> 0 us
    all_to_all x1 -> x0, blocking collectives: 185 us -> none  [per_device(): lax.all_to_all(outgoing, 'ctx', split_axis=0, concat_axis=0, tiled=True)]
    pallas_call x0 -> x1, Pallas kernels: none -> 121 us  [per_device(): pl.pallas_call(kernel, out_shape=shapes, in_specs=[vmem] * 6 + [hbm] + [v...]
    unnamed x5 -> x0, waiting for transfers between devices: 115 us -> none
    all_gather x1 -> x0, waiting for transfers between devices: 95.4 us -> none  [per_device(): whole_keys = lax.all_gather(key_values, 'ctx', axis=0, tiled=True)]
    all_to_all x1 -> x0, waiting for transfers between devices: 72.2 us -> none  [per_device(): lax.all_to_all(partial_rows.astype(jnp.bfloat16), 'ctx', split_axis=0, co...]
    dot_general x9 -> x0, matrix products: 38 us -> none  [the longest x1 10.2 us: per_device(): lax.dot_general(grad_up, w_up, contract, preferred_element_type=jnp.float32)]
    all_to_all x2 -> x0, local copies, waits for them, and re-layouts: 17.5 us -> none  [the longest x1 8.76 us: per_device(): lax.all_to_all(outgoing, 'ctx', split_axis=0, concat_axis=0, tiled=True)]
    reduce_sum x4 -> x0, other arithmetic: 14.9 us -> none  [the longest x1 7.05 us: per_device(): jnp.sum(returned.astype(jnp.float32).reshape(EXPERTS, copies, capacity, m...]
  transfers between devices with their start and end apart: 4 -> 0, of which waited for: 4 -> 0; matrix products, arithmetic and copies ran while one was open for 8% -> 0% of each run, Pallas kernels for 0% -> 0%
where the time goes in v1:
time: 131 us
  Pallas kernels  121 us (92%)
  local copies, waits for them, and re-layouts  8.66 us (7%)
    pallas_call x1, Pallas kernels, per_device(): pl.pallas_call(kernel, out_shape=shapes, in_specs=[vmem] * 6 + [hbm] + [v...  121 us
    unnamed x6, local copies, waits for them, and re-layouts  8.66 us

profile of v1, /device:TPU:1, one launch (start us, length us, event | category | flops | bytes accessed | tf_op | source)
XLA Modules:
  0.0 130.8 jit_solution(13343508289228283661)
XLA Ops:
  0.6 1.4 %copy.18.ids_ref = s32[128,2]{1,0:T(8,128)} copy(s32[128,2]{0,1:T(2,128)} %param.21) | data formatting | bytes 2048 | tf_op args[7]
  2.0 1.4 %copy.19.rw_ref = f32[128,2]{1,0:T(8,128)} copy(f32[128,2]{0,1:T(2,128)} %param.22) | data formatting | bytes 2048 | tf_op args[8]
  3.5 121.5 %shard_map.165 = (bf16[128,384]{1,0:T(8,128)(2,1)}, bf16[128,128]{1,0:T(8,128)(2,1)}, bf16[128,128]{1,0:T(8,128)(2,1)}, bf16[128,384]{1,0:T(8,128)(2,1)}) custom-call(bf16[128,384]{1,0:T(8,128)(2,1)} %q_ref.1, bf16[128,128]{1,0:T(8,128)(2,1)} %k_ref.1, bf16[128,128]{1,0:T(8,128)(2,1)} %v_ref.1, bf16[128,384]{1,0:T(8,128)(2,1)} %ao_ref.1, ...), custom_call_target="tpu_custom_call" | custom-call | flops 12999999488 | bytes 12000000 | tf_op jit(solution)/shard_map/pallas_call | solution.py:521
  124.9 1.5 %copy.24 = bf16[128,384]{1,0:T(8,128)(2,1)} copy(bf16[128,384]{1,0:T(8,128)(2,1)} %get-tuple-element.8) | data formatting | bytes 196608
  126.5 1.4 %copy.25 = bf16[128,128]{1,0:T(8,128)(2,1)} copy(bf16[128,128]{1,0:T(8,128)(2,1)} %get-tuple-element.9) | data formatting | bytes 65536
  127.8 1.4 %copy.26 = bf16[128,128]{1,0:T(8,128)(2,1)} copy(bf16[128,128]{1,0:T(8,128)(2,1)} %get-tuple-element.10) | data formatting | bytes 65536
  129.2 1.5 %copy.27 = bf16[128,384]{1,0:T(8,128)(2,1)} copy(bf16[128,384]{1,0:T(8,128)(2,1)} %get-tuple-element.11) | data formatting | bytes 196608

commit v2 on v1

v2 whole, which is shorter than its diff:
```python
import jax
import jax.numpy as jnp
import numpy as np
from jax import lax
from jax.experimental import pallas as pl
from jax.experimental.pallas import tpu as pltpu
from jax.sharding import PartitionSpec as P

EXPERTS = 8
HEAD = 128
CAP = 36
THIRD = 12
TILE = 16
SPREAD = 8 * TILE
CT = 128
N_CTX = 32
HEADS = 3
WINDOW = 10
CHIPS = 16
SUBS = 3
SUB = 96
Y_LAST = ()
BLOCK = 288
SET = 144
COLS = 384
HALF = 1536
WIDE = 3072
HID = 512
MESH = pl.DeviceIdType.MESH
F32 = jnp.float32
BF16 = jnp.bfloat16
NT = (((1,), (1,)), ((), ()))
NN = (((1,), (0,)), ((), ()))
TN = (((0,), (0,)), ((), ()))


def dot(a, b, dims):
    return lax.dot_general(a, b, dims, preferred_element_type=F32)


def kernel(
    q_ref, k_ref, v_ref, ao_ref, go_ref, seg_ref, gm_ref, ids_ref, rw_ref,
    sg_ref, su_ref, perm_ref, wg_ref, wu_ref, wd_ref,
    dq_ref, dk_ref, dv_ref, dm_ref,
    kv, st, q3, g3, dkv, dks, dacc,
    gm, packed, arrive, arr, sgr, sur, perm, sg, su, sgx, sux, wg, wu, wd,
    part, b1, b2, b3s, b3, unpacked, ret,
    ld_sem, kv_s, kv_r, kf_s, kf_r, ds_s, ds_r, da_s, da_r,
    pa_s, pa_r, g1_s, g1_r, g2_s, g2_r, g3_s, g3_r, w_s, w_r,
    x_s, x_r, r1_s, r1_r, r2_s, r2_r, r3_s, r3_r, pr_s, pr_r,
):
    c = lax.axis_index("ctx")
    u = lax.axis_index("tp")
    core = c % 2
    chip = c // 2
    zp = chip % 2
    xh = u // 4
    y = u % 4
    quarter = c % 4
    sibling = (c + 1 - 2 * core, u)
    first = (c + core * (2 - 4 * zp), u + (1 - core) * (4 - 8 * xh))
    last = (c + (1 - core) * (2 - 4 * zp), u + core * (4 - 8 * xh))

    def along_y(dy):
        return (c, xh * 4 + (y + dy) % 4)

    def send(src, dst, ss, rs, to):
        pltpu.make_async_remote_copy(
            src_ref=src, dst_ref=dst, send_sem=ss, recv_sem=rs,
            device_id=to, device_id_type=MESH,
        ).start()

    def got(dst, ss, rs):
        pltpu.make_async_remote_copy(
            src_ref=dst, dst_ref=dst, send_sem=ss, recv_sem=rs,
            device_id=sibling, device_id_type=MESH,
        ).wait_recv()

    def sent(src, ss, rs):
        pltpu.make_async_remote_copy(
            src_ref=src, dst_ref=src, send_sem=ss, recv_sem=rs,
            device_id=sibling, device_id_type=MESH,
        ).wait_send()

    barrier = pltpu.get_barrier_semaphore()

    for i in range(1, N_CTX):
        pl.semaphore_signal(
            barrier, inc=1, device_id=((c + i) % N_CTX, u), device_id_type=MESH
        )
    for dy in (1, 2, 3):
        pl.semaphore_signal(barrier, inc=1, device_id=along_y(dy), device_id_type=MESH)
    pl.semaphore_signal(
        barrier, inc=1, device_id=(c, u + 4 - 8 * xh), device_id_type=MESH
    )

    own_cols = pl.ds(pl.multiple_of(u * COLS, 128), COLS)
    expert = c // 4
    rank_pair = expert % 4
    loads = [(gm_ref.at[:, own_cols], gm), (perm_ref, perm)]
    for x in (0, 1):
        for diff in range(4):
            group = 4 * x + (rank_pair + 4 - diff) % 4
            loads += [(sg_ref.at[group], sgr.at[x, diff]), (su_ref.at[group], sur.at[x, diff])]
    weights = [(wd_ref, wd.at[core]), (wg_ref, wg.at[core]), (wu_ref, wu.at[core])]
    loads += weights

    def load(i):
        return pltpu.make_async_copy(loads[i][0], loads[i][1], ld_sem.at[i])

    for i in range(len(loads)):
        load(i).start()

    ids = ids_ref[...]
    expert_row = lax.broadcasted_iota(jnp.int32, (EXPERTS, CT), 0)
    hot = [(ids[k : k + 1, :] == expert_row).astype(F32) for k in range(2)]
    before = (
        lax.broadcasted_iota(jnp.int32, (CT, CT), 0) < lax.broadcasted_iota(jnp.int32, (CT, CT), 1)
    ).astype(BF16)
    rank = dot((hot[0] + hot[1]).astype(BF16), before, NN)
    third = (rank >= THIRD).astype(F32) + (rank >= 2 * THIRD).astype(F32)
    place = rank + (SPREAD - THIRD) * third + (TILE * expert_row).astype(F32)
    slot_row = lax.broadcasted_iota(jnp.int32, (SUBS * SPREAD, CT), 0)
    pick = []
    for k in range(2):
        slot = jnp.sum(hot[k] * place, axis=0, keepdims=True).astype(jnp.int32)
        pick.append((slot_row == slot).astype(F32))
    selector = (pick[0] + pick[1]).astype(BF16)
    load(0).wait()
    packed[...] = dot(selector, gm[...], NN).astype(BF16).reshape(SUBS, EXPERTS, TILE, COLS)
    kv[0, core, :, :HEAD] = k_ref[...]
    kv[0, core, :, HEAD:] = v_ref[...]

    pl.semaphore_wait(barrier, N_CTX - 1 + 4)

    own_x = c // 16
    own_pair = (chip % 8) // 2
    for s in range(SUBS):

        @pl.loop(0, EXPERTS)
        def _(e):
            diff = (e % 4 - own_pair + 4) % 4
            to_z = (1 - zp) * (diff // 2) + zp * (((diff + 1) // 2 + 1) % 2)
            slot = 4 * own_x + (1 - zp) * (diff % 2) + zp * (2 + diff // 2)
            to = ((e // 4) * 8 + 2 * (e % 4) + to_z) * 2 + core

            @pl.when(e == expert)
            def _():
                pltpu.make_async_copy(
                    packed.at[s, e], arrive.at[s, slot], pa_r.at[s, slot]
                ).start()

            @pl.when(e != expert)
            def _():
                send(
                    packed.at[s, e], arrive.at[s, slot],
                    pa_s.at[s, e], pa_r.at[s, slot], (to, u),
                )

    later = jnp.minimum(WINDOW, CHIPS - 1 - chip) + 1
    earlier = jnp.minimum(WINDOW, chip) + 1

    send(kv.at[0, core], kv.at[0, core], kf_s.at[0], kf_r.at[0], sibling)

    @pl.loop(1, later)
    def _(d):
        send(kv.at[0, core], kv.at[d, core], kv_s.at[d], kv_r.at[d], (c + 2 * d, u))

    for i, (src, dst) in enumerate(weights):
        send(src, dst, w_s.at[i], w_r.at[i], sibling)

    q3[...] = jnp.concatenate([q_ref[:, h * HEAD : (h + 1) * HEAD] for h in range(HEADS)], axis=0)
    g3[...] = jnp.concatenate([go_ref[:, h * HEAD : (h + 1) * HEAD] for h in range(HEADS)], axis=0)
    a3 = jnp.concatenate([ao_ref[:, h * HEAD : (h + 1) * HEAD] for h in range(HEADS)], axis=0)
    row_dots = jnp.sum(
        jnp.transpose(g3[...].astype(F32) * a3.astype(F32)), axis=0, keepdims=True
    )
    segs = seg_ref[...]
    starts = [
        jnp.sum((segs < k).astype(F32)).astype(jnp.int32) for k in (1, 2)
    ]
    own_seg = seg_ref[pl.ds(c, 1), :]
    start = jnp.where(own_seg == 0, 0, jnp.where(own_seg == 1, starts[0], starts[1]))
    start = jnp.concatenate([start] * HEADS, axis=1)
    own_pos = c * CT + lax.broadcasted_iota(jnp.int32, (1, CT), 1)
    own_pos = jnp.concatenate([own_pos] * HEADS, axis=1)

    def order_saved():
        for i in range(1, 18):
            load(i).wait()
        for raw, ordered in ((sgr, sg), (sur, su)):
            for x in (0, 1):
                rows = dot(perm[...], raw[x].reshape(4 * SET, HID), NN).astype(BF16)
                ordered[:, :, :, x] = rows.reshape(2, 2, SUBS, SUB // 2, HID)
        for i, (src, dst) in enumerate(((sg, sgx), (su, sux))):
            for j in (0, 1):
                send(src.at[j, 1 - core], dst.at[j], x_s.at[i, j], x_r.at[i, j], sibling)

    def dense_map(shape, row_axis):
        rows = lax.broadcasted_iota(jnp.int32, shape, row_axis)
        slots = lax.broadcasted_iota(jnp.int32, shape, 1 - row_axis)
        group = sum((rows >= THIRD * i).astype(jnp.int32) for i in range(1, 8))
        return (slots == rows + (TILE - THIRD) * group).astype(BF16)

    def dense(s):
        @pl.loop(0, 8)
        def _(i):
            got(arrive.at[s, i], pa_s.at[s, i], pa_r.at[s, i])

        arr[zp, s * SUB : (s + 1) * SUB, own_cols] = dot(
            dense_map((SUB, SPREAD), 0), arrive[s].reshape(SPREAD, COLS), NN
        ).astype(BF16)

    def at_block(fr, lr):
        dz = lr * (1 - core) + fr * core
        dx = fr * (1 - core) + lr * core
        return zp + dz * (1 - 2 * zp), xh + dx * (1 - 2 * xh)

    def piece(ref, s, fr, lr, py):
        row, col = at_block(fr, lr)
        return ref.at[
            row, pl.ds(s * SUB, SUB), pl.ds(pl.multiple_of(col * HALF + py * COLS, 128), COLS)
        ]

    def y_at(dy):
        return (y + dy) % 4

    def to_last(s, fr, dy):
        mine = piece(arr, s, fr, 0, y_at(4 - dy))
        send(mine, mine, g3_s.at[s, fr, dy], g3_r.at[s, fr, dy], last)

    def to_y(s, fr, lr):
        mine = piece(arr, s, fr, lr, y)
        for dy in (1, 2, 3):
            send(mine, mine, g2_s.at[s, fr, lr, dy], g2_r.at[s, fr, lr, dy], along_y(dy))

    def from_y(s, fr, lr, dy):
        got(
            piece(arr, s, fr, lr, y_at(4 - dy)),
            g2_s.at[s, fr, lr, dy], g2_r.at[s, fr, lr, dy],
        )

    def from_last(s, fr, dy):
        got(piece(arr, s, fr, 1, y_at(4 - dy)), g3_s.at[s, fr, dy], g3_r.at[s, fr, dy])

    def gather_1(s):
        dense(s)
        mine = piece(arr, s, 0, 0, y)
        send(mine, mine, g1_s.at[s], g1_r.at[s], first)
        to_y(s, 0, 0)
        to_last(s, 0, 0)

    def gather_2(s):
        got(piece(arr, s, 1, 0, y), g1_s.at[s], g1_r.at[s])
        to_y(s, 1, 0)
        to_last(s, 1, 0)

    def gather_3(s):
        for fr in (0, 1):
            if s in Y_LAST:
                from_last(s, fr, 0)
                to_y(s, fr, 1)
            else:
                for dy in (1, 2, 3):
                    from_y(s, fr, 0, dy)
                    to_last(s, fr, dy)

    def gather_4(s):
        for fr in (0, 1):
            for lr in (0, 1) if s in Y_LAST else (1,):
                for dy in range(4):
                    if s not in Y_LAST:
                        from_last(s, fr, dy)
                    elif dy > 0:
                        from_y(s, fr, lr, dy)

    def wait_weights():
        for i in range(18, 21):
            load(i).wait()
        for i, (src, _) in enumerate(weights):
            got((wd, wg, wu)[i].at[1 - core], w_s.at[i], w_r.at[i])
        for i, dst in enumerate((sgx, sux)):
            for j in (0, 1):
                got(dst.at[j], x_s.at[i, j], x_r.at[i, j])

    def expert_rows(s):
        rows = pl.ds(s * SUB, SUB)
        grads = []
        for k, gate, up in (
            (core, sg[:, core, s], su[:, core, s]),
            (1 - core, sgx[:, s], sux[:, s]),
        ):
            hidden = dot(arr[:, rows, :].reshape(2 * SUB, WIDE), wd[k], NT)
            gate = gate.reshape(2 * SUB, HID).astype(F32)
            up = up.reshape(2 * SUB, HID).astype(F32)
            sig = jax.nn.sigmoid(gate)
            hs = hidden * sig
            grad_up = (hs * gate).astype(BF16)
            grad_gate = (hs * up * (1.0 + gate * (1.0 - sig))).astype(BF16)
            grads.append((k, grad_gate, grad_up))

        @pl.loop(0, WIDE // HID)
        def _(n):
            cols = pl.ds(pl.multiple_of(n * HID, HID), HID)
            out = sum(
                dot(grad_gate, wg[k, cols, :], NT) + dot(grad_up, wu[k, cols, :], NT)
                for k, grad_gate, grad_up in grads
            )
            part[:, rows, cols] = out.astype(BF16).reshape(2, SUB, HID)

    def part_at(s, fr, lr, py):
        row, col = at_block(fr, lr)
        cols = pl.ds(pl.multiple_of(col * HALF + py * COLS, 128), COLS)
        return part[row, pl.ds(s * SUB, SUB), cols].astype(F32)

    def half_to_last(s, fr, dy):
        mine = piece(part, s, fr, 1, y_at(dy))
        send(mine, b1.at[s, fr, dy], r1_s.at[s, fr, dy], r1_r.at[s, fr, dy], last)

    def half_to_y(s, fr, lr, dy):
        send(
            piece(part, s, fr, lr, y_at(dy)), b2.at[s, fr, lr, dy - 1],
            r2_s.at[s, fr, lr, dy], r2_r.at[s, fr, lr, dy], along_y(dy),
        )

    def add_last(s, fr, dy):
        got(b1.at[s, fr, dy], r1_s.at[s, fr, dy], r1_r.at[s, fr, dy])
        return b1[s, fr, dy].astype(F32)

    def add_y(s, fr, lr):
        total = part_at(s, fr, lr, y)
        for dy in (1, 2, 3):
            got(b2.at[s, fr, lr, dy - 1], r2_s.at[s, fr, lr, dy], r2_r.at[s, fr, lr, dy])
            total = total + b2[s, fr, lr, dy - 1].astype(F32)
        return total

    def return_1(s):
        if s in Y_LAST:
            for lr in (1, 0):
                for fr in (1, 0):
                    for dy in (1, 2, 3):
                        half_to_y(s, fr, lr, dy)
        else:
            for dy in (1, 2, 3, 0):
                for fr in (1, 0):
                    half_to_last(s, fr, dy)

    def return_2(s):
        for fr in (1, 0):
            if s in Y_LAST:
                mine = piece(part, s, fr, 1, y)
                mine[...] = add_y(s, fr, 1).astype(BF16)
                half_to_last(s, fr, 0)
            else:
                for dy in (1, 2, 3):
                    mine = piece(part, s, fr, 0, y_at(dy))
                    total = part_at(s, fr, 0, y_at(dy)) + add_last(s, fr, dy)
                    mine[...] = total.astype(BF16)
                    half_to_y(s, fr, 0, dy)

    def return_3(s):
        b3s[s] = (add_y(s, 1, 0) + add_last(s, 1, 0)).astype(BF16)
        send(b3s.at[s], b3.at[s], r3_s.at[s], r3_r.at[s], first)

    def return_4(s):
        total = add_y(s, 0, 0) + add_last(s, 0, 0)
        got(b3.at[s], r3_s.at[s], r3_r.at[s])
        rows = (total + b3[s].astype(F32)).astype(BF16)
        unpacked[s] = (
            dot(dense_map((SPREAD, SUB), 1), rows, NN).astype(BF16).reshape(8, TILE, COLS)
        )

        @pl.loop(0, 8)
        def _(i):
            to = source_of(i)

            @pl.when(to == c)
            def _():
                pltpu.make_async_copy(
                    unpacked.at[s, i], ret.at[s, expert], pr_r.at[s, expert]
                ).start()

            @pl.when(to != c)
            def _():
                send(
                    unpacked.at[s, i], ret.at[s, expert],
                    pr_s.at[s, i], pr_r.at[s, expert], (to, u),
                )

    def source_of(i):
        at = i % 4
        from_z = at // 2
        diff = (1 - zp) * (at - from_z) + zp * ((at + 2) * (1 - from_z) + 3 * from_z * (at % 2))
        return ((i // 4) * 8 + 2 * ((rank_pair + 4 - diff) % 4) + from_z) * 2 + core

    def keys_forward():
        @pl.loop(1, earlier)
        def _(d):
            mine = kv.at[d, core]
            got(mine, kv_s.at[d], kv_r.at[d])
            send(mine, mine, kf_s.at[d], kf_r.at[d], sibling)

    def keys_of(d):
        return kv[d, :, :, :HEAD].reshape(2 * CT, HEAD)

    def scores_pass():
        def step(d, top):
            got(kv.at[d, 1 - core], kf_s.at[d], kf_r.at[d])
            s = dot(keys_of(d), q3[...], NT) * (HEAD ** -0.5)
            pos = (chip - d) * 2 * CT + lax.broadcasted_iota(jnp.int32, (2 * CT, 1), 0)
            s = jnp.where((pos <= own_pos) & (pos >= start), s, -1e30)
            st[d] = s
            return jnp.maximum(top, jnp.max(s, axis=0, keepdims=True))

        top = lax.fori_loop(0, earlier, step, jnp.full((1, HEADS * CT), -1e30, F32))

        def step_2(d, total):
            p = jnp.exp(st[d] - top)
            st[d] = p
            return total + jnp.sum(p, axis=0, keepdims=True)

        total = lax.fori_loop(0, earlier, step_2, jnp.zeros((1, HEADS * CT), F32))
        return 1.0 / total

    def grads_pass(inverse):
        def step(d, dqt):
            probs = st[d] * inverse
            keys = keys_of(d)
            values = kv[d, :, :, HEAD:].reshape(2 * CT, HEAD)
            grad_probs = dot(values, g3[...], NT)
            grad_scores = (probs * (grad_probs - row_dots)).astype(BF16)
            dkv[d, :, :, :HEAD] = (
                (dot(grad_scores, q3[...], NN) * (HEAD ** -0.5)).astype(BF16).reshape(2, CT, HEAD)
            )
            dkv[d, :, :, HEAD:] = (
                dot(probs.astype(BF16), g3[...], NN).astype(BF16).reshape(2, CT, HEAD)
            )
            send(dkv.at[d, 1 - core], dks.at[d], ds_s.at[d], ds_r.at[d], sibling)
            return dqt + dot(keys, grad_scores, TN)

        dqt = lax.fori_loop(0, earlier, step, jnp.zeros((HEAD, HEADS * CT), F32))
        dq = jnp.transpose(dqt * (HEAD ** -0.5)).astype(BF16)
        for h in range(HEADS):
            dq_ref[:, h * HEAD : (h + 1) * HEAD] = dq[h * CT : (h + 1) * CT, :]

    def keys_return():
        @pl.loop(0, earlier)
        def _(d):
            got(dks.at[d], ds_s.at[d], ds_r.at[d])
            dkv[d, core] = (dkv[d, core].astype(F32) + dks[d].astype(F32)).astype(BF16)

            @pl.when(d > 0)
            def _():
                send(dkv.at[d, core], dacc.at[d], da_s.at[d], da_r.at[d], (c - 2 * d, u))

    def keys_finish():
        def step(d, total):
            got(dacc.at[d], da_s.at[d], da_r.at[d])
            return total + dacc[d].astype(F32)

        total = lax.fori_loop(1, later, step, dkv[0, core].astype(F32))
        dk_ref[...] = total[:, :HEAD].astype(BF16)
        dv_ref[...] = total[:, HEAD:].astype(BF16)

    order_saved()
    gather_1(0)
    gather_1(1)
    gather_2(0)
    gather_1(2)
    gather_2(1)
    gather_2(2)
    gather_3(0)
    keys_forward()
    gather_3(1)
    gather_3(2)
    gather_4(0)
    wait_weights()
    expert_rows(0)
    return_1(0)
    gather_4(1)
    expert_rows(1)
    return_1(1)
    inverse = scores_pass()
    return_2(0)
    gather_4(2)
    expert_rows(2)
    return_1(2)
    grads_pass(inverse)
    return_2(1)
    return_3(0)
    return_2(2)
    keys_return()
    return_4(0)
    return_3(1)
    return_4(1)
    return_3(2)
    return_4(2)
    keys_finish()

    for s in range(SUBS):
        sent(b3s.at[s], g1_s.at[s], g1_r.at[s])
        sent(b3s.at[s], r3_s.at[s], r3_r.at[s])
        for fr in (0, 1):
            for dy in range(1 if s in Y_LAST else 4):
                sent(b3s.at[s], g3_s.at[s, fr, dy], g3_r.at[s, fr, dy])
                sent(b3s.at[s], r1_s.at[s, fr, dy], r1_r.at[s, fr, dy])
            for lr in (0, 1) if s in Y_LAST else (0,):
                for dy in (1, 2, 3):
                    sent(b3s.at[s], g2_s.at[s, fr, lr, dy], g2_r.at[s, fr, lr, dy])
                    sent(b3s.at[s], r2_s.at[s, fr, lr, dy], r2_r.at[s, fr, lr, dy])
    for i, (_, dst) in enumerate(weights):
        sent(dst, w_s.at[i], w_r.at[i])
    for i, src in enumerate((sgx, sux)):
        for j in (0, 1):
            sent(src.at[j], x_s.at[i, j], x_r.at[i, j])
    sent(kv.at[0, core], kf_s.at[0], kf_r.at[0])
    sent(dkv.at[0, core], ds_s.at[0], ds_r.at[0])

    @pl.loop(1, later)
    def _(d):
        sent(kv.at[0, core], kv_s.at[d], kv_r.at[d])

    @pl.loop(1, earlier)
    def _(d):
        sent(kv.at[d, core], kf_s.at[d], kf_r.at[d])
        sent(dkv.at[d, 1 - core], ds_s.at[d], ds_r.at[d])
        sent(dkv.at[d, core], da_s.at[d], da_r.at[d])

    for s in range(SUBS):

        @pl.loop(0, 8)
        def _(i):
            @pl.when(i != expert)
            def _():
                sent(packed.at[s, i], pa_s.at[s, i], pa_r.at[s, i])

            @pl.when(source_of(i) != c)
            def _():
                sent(unpacked.at[s, i], pr_s.at[s, i], pr_r.at[s, i])

        @pl.loop(0, EXPERTS)
        def _(i):
            got(ret.at[s, i], pr_s.at[s, i], pr_r.at[s, i])

    rows = ret[...].reshape(SUBS * SPREAD, COLS)
    total = jnp.zeros((CT, COLS), F32)
    for k in range(2):
        weight = jnp.transpose(jnp.broadcast_to(rw_ref[k : k + 1, :], (CT, CT)))[:, :1]
        total = total + weight * dot(pick[k].astype(BF16), rows, TN)
    dm_ref[...] = total.astype(BF16)


def finish(*refs):
    for src, dst in zip(refs[:4], refs[4:]):
        dst[...] = src[...]


def per_device(
    queries, key_rows, value_rows, attn_out, grad_out, segments, grad_moe_out,
    expert_ids, route_weights, saved_gate, saved_up, w_gate, w_up, w_down,
):
    order = np.zeros((4, SUBS, 4, THIRD, 4, 4, CAP), np.float32)
    for part in range(4):
        for at in range(4):
            diff = ((0, 1, 1, 2), (2, 3, 0, 3))[part // 2][at]
            for s in range(SUBS):
                for i in range(THIRD):
                    order[part, s, at, i, diff, 2 * (at // 2) + part % 2, THIRD * s + i] = 1
    order = jnp.asarray(order.reshape(4 * SET, 4 * SET), BF16)
    vmem = pl.BlockSpec(memory_space=pltpu.VMEM)
    hbm = pl.BlockSpec(memory_space=pl.ANY)
    dma = pltpu.SemaphoreType.DMA
    slots = WINDOW + 1
    shapes = [
        jax.ShapeDtypeStruct((CT, HEADS * HEAD), BF16),
        jax.ShapeDtypeStruct((CT, HEAD), BF16),
        jax.ShapeDtypeStruct((CT, HEAD), BF16),
        jax.ShapeDtypeStruct((CT, COLS), BF16),
    ]
    scratch = [
        pltpu.VMEM((slots, 2, CT, 2 * HEAD), BF16),
        pltpu.VMEM((slots, 2 * CT, HEADS * CT), F32),
        pltpu.VMEM((HEADS * CT, HEAD), BF16),
        pltpu.VMEM((HEADS * CT, HEAD), BF16),
        pltpu.VMEM((slots, 2, CT, 2 * HEAD), BF16),
        pltpu.VMEM((slots, CT, 2 * HEAD), BF16),
        pltpu.VMEM((slots, CT, 2 * HEAD), BF16),
        pltpu.VMEM((CT, COLS), BF16),
        pltpu.VMEM((SUBS, EXPERTS, TILE, COLS), BF16),
        pltpu.VMEM((SUBS, 8, TILE, COLS), BF16),
        pltpu.VMEM((2, BLOCK, WIDE), BF16),
        pltpu.VMEM((2, 4, SET, HID), BF16),
        pltpu.VMEM((2, 4, SET, HID), BF16),
        pltpu.VMEM((4 * SET, 4 * SET), BF16),
        pltpu.VMEM((2, 2, SUBS, 2, SUB // 2, HID), BF16),
        pltpu.VMEM((2, 2, SUBS, 2, SUB // 2, HID), BF16),
        pltpu.VMEM((2, SUBS, 2, SUB // 2, HID), BF16),
        pltpu.VMEM((2, SUBS, 2, SUB // 2, HID), BF16),
        pltpu.VMEM((2, WIDE, HID), BF16),
        pltpu.VMEM((2, WIDE, HID), BF16),
        pltpu.VMEM((2, HID, WIDE), BF16),
        pltpu.VMEM((2, BLOCK, WIDE), BF16),
        pltpu.VMEM((SUBS, 2, 4, SUB, COLS), BF16),
        pltpu.VMEM((SUBS, 2, 2, 3, SUB, COLS), BF16),
        pltpu.VMEM((SUBS, SUB, COLS), BF16),
        pltpu.VMEM((SUBS, SUB, COLS), BF16),
        pltpu.VMEM((SUBS, 8, TILE, COLS), BF16),
        pltpu.VMEM((SUBS, EXPERTS, TILE, COLS), BF16),
        dma((21,)),
    ]
    for shape in (
        (slots,), (slots,), (slots,), (slots,),
        (SUBS, 8),
        (SUBS,), (SUBS, 2, 2, 4), (SUBS, 2, 4), (3,),
        (2, 2), (SUBS, 2, 4), (SUBS, 2, 2, 4), (SUBS,),
        (SUBS, 8),
    ):
        scratch += [dma(shape), dma(shape)]
    results = pl.pallas_call(
        kernel,
        out_shape=shapes,
        in_specs=[vmem] * 6 + [hbm] + [vmem] * 2 + [hbm] * 6,
        out_specs=[vmem] * 4,
        scratch_shapes=scratch,
        compiler_params=pltpu.CompilerParams(
            collective_id=0, has_side_effects=True, vmem_limit_bytes=60 * 2**20
        ),
        cost_estimate=pl.CostEstimate(
            flops=13 * 10**9, bytes_accessed=12 * 10**6, transcendentals=2 * 10**6
        ),
    )(
        queries, key_rows, value_rows, attn_out, grad_out,
        segments.reshape(N_CTX, CT), grad_moe_out, expert_ids.T, route_weights.T,
        saved_gate.reshape(8, SET, HID), saved_up.reshape(8, SET, HID), order,
        w_gate, w_up, w_down,
    )
    return pl.pallas_call(
        finish, out_shape=shapes, in_specs=[vmem] * 4, out_specs=[vmem] * 4
    )(*results)


def solution(mesh):
    in_specs = (
        P("ctx", "tp"), P("ctx", "tp"), P("ctx", "tp"), P("ctx", "tp"), P("ctx", "tp"),
        P(), P("ctx", None), P("ctx", None), P("ctx", None),
        P("ctx", "tp"), P("ctx", "tp"),
        P(None, ("ctx", "tp")), P(None, ("ctx", "tp")), P(("ctx", "tp"), None),
    )
    out_specs = (P("ctx", "tp"), P("ctx", "tp"), P("ctx", "tp"), P("ctx", "tp"))
    return jax.shard_map(
        per_device, mesh=mesh, in_specs=in_specs, out_specs=out_specs, check_vma=False
    )
```

time: 131 us -> 111 us (0.85)
  Pallas kernels: 121 us -> 111 us
  local copies, waits for them, and re-layouts: 8.66 us -> 0 us
    pallas_call x1, Pallas kernels: 121 us -> 109 us  [per_device(): pl.pallas_call(kernel, out_shape=shapes, in_specs=[vmem] * 6 + [hbm] + [v...]
    unnamed x6 -> x0, local copies, waits for them, and re-layouts: 8.66 us -> none
    pallas_call x0 -> x1, Pallas kernels: none -> 1.68 us  [per_device(): pl.pallas_call(finish, out_shape=shapes, in_specs=[vmem] * 4, out_specs=[...]
where the time goes in v2:
time: 111 us
  Pallas kernels  111 us (100%)
    pallas_call x1, Pallas kernels, per_device(): pl.pallas_call(kernel, out_shape=shapes, in_specs=[vmem] * 6 + [hbm] + [v...  109 us

profile of v2, /device:TPU:1, one launch (start us, length us, event | category | flops | bytes accessed | tf_op | source)
XLA Modules:
  0.0 111.2 jit_solution(5496542248634128107)
XLA Ops:
  0.6 108.9 %shard_map.174 = (bf16[128,384]{1,0:T(8,128)(2,1)}, bf16[128,128]{1,0:T(8,128)(2,1)}, bf16[128,128]{1,0:T(8,128)(2,1)}, bf16[128,384]{1,0:T(8,128)(2,1)}) custom-call(bf16[128,384]{1,0:T(8,128)(2,1)} %q_ref.1, bf16[128,128]{1,0:T(8,128)(2,1)} %k_ref.1, bf16[128,128]{1,0:T(8,128)(2,1)} %v_ref.1, bf16[128,384]{1,0:T(8,128)(2,1)} %ao_ref.1, ...), custom_call_target="tpu_custom_call" | custom-call | flops 12999999488 | bytes 12000000 | tf_op jit(solution)/shard_map/pallas_call | solution.py:619
  109.5 1.7 %shard_map.175 = (bf16[128,384]{1,0:T(8,128)(2,1)}, bf16[128,128]{1,0:T(8,128)(2,1)}, bf16[128,128]{1,0:T(8,128)(2,1)}, bf16[128,384]{1,0:T(8,128)(2,1)}) custom-call(bf16[128,384]{1,0:T(8,128)(2,1)} %get-tuple-element.8.refs_0_, bf16[128,128]{1,0:T(8,128)(2,1)} %get-tuple-element.9.refs_1_, bf16[128,128]{1,0:T(8,128)(2,1)} %get-tuple-element.10.refs_2_, ...), custom_call_target="tpu_custom_call" | custom-call | tf_op jit(solution)/shard_map/pallas_call | solution.py:637

commit v3 on v2

--- a/solution.py
+++ b/solution.py
@@ -19,7 +19,7 @@
 CHIPS = 16
 SUBS = 3
 SUB = 96
-Y_LAST = ()
+Y_LAST = (2,)
 BLOCK = 288
 SET = 144
 COLS = 384

time: 111 us -> 110 us (level)
  the two profiles are of different devices: /device:TPU:1 before, /device:TPU:24 now
where the time goes in v3:
time: 110 us; the launch traced here: 109 us
  Pallas kernels  109 us (99%)
    pallas_call x1, Pallas kernels, per_device(): pl.pallas_call(kernel, out_shape=shapes, in_specs=[vmem] * 6 + [hbm] + [v...  107 us

profile of v3, /device:TPU:24, one launch (start us, length us, event | category | flops | bytes accessed | tf_op | source)
XLA Modules:
  0.0 109.4 jit_solution(16356105845263335266)
XLA Ops:
  0.6 107.0 %shard_map.174 = (bf16[128,384]{1,0:T(8,128)(2,1)}, bf16[128,128]{1,0:T(8,128)(2,1)}, bf16[128,128]{1,0:T(8,128)(2,1)}, bf16[128,384]{1,0:T(8,128)(2,1)}) custom-call(bf16[128,384]{1,0:T(8,128)(2,1)} %q_ref.1, bf16[128,128]{1,0:T(8,128)(2,1)} %k_ref.1, bf16[128,128]{1,0:T(8,128)(2,1)} %v_ref.1, bf16[128,384]{1,0:T(8,128)(2,1)} %ao_ref.1, ...), custom_call_target="tpu_custom_call" | custom-call | flops 12999999488 | bytes 12000000 | tf_op jit(solution)/shard_map/pallas_call | solution.py:619
  107.7 1.7 %shard_map.175 = (bf16[128,384]{1,0:T(8,128)(2,1)}, bf16[128,128]{1,0:T(8,128)(2,1)}, bf16[128,128]{1,0:T(8,128)(2,1)}, bf16[128,384]{1,0:T(8,128)(2,1)}) custom-call(bf16[128,384]{1,0:T(8,128)(2,1)} %get-tuple-element.8.refs_0_, bf16[128,128]{1,0:T(8,128)(2,1)} %get-tuple-element.9.refs_1_, bf16[128,128]{1,0:T(8,128)(2,1)} %get-tuple-element.10.refs_2_, ...), custom_call_target="tpu_custom_call" | custom-call | tf_op jit(solution)/shard_map/pallas_call | solution.py:637
